TPU v7x, 32 devices: a whole 2x2x4 slice. The times are simulated.
32 devices in a mesh: freq: 2 (over y), mid: 4 (over z), off: 4 (over x, core).
Axes of the slice: x: 2, y: 2, z: 4, core: 2. Of those that a mesh axis runs over, the one named last changes fastest.
Arguments:
- observed: bfloat16 [4, 8192, 8192], P('freq', 'mid', 'off'), parts along dimension 0, may hold values from -6 to 6
- trace_mask: int32 [8192, 8192], P('mid', 'off'), may hold values 0 or 1
- left_factor: bfloat16 [4, 8192, 256], P('freq', ('mid', 'off')), parts along dimension 0, may hold values from -1.5 to 1.5
- right_factor: bfloat16 [4, 8192, 256], P('freq', ('off', 'mid')), parts along dimension 0, may hold values from -1.5 to 1.5
Outputs:
- left_next: float32 [4, 8192, 256], P('freq', ('mid', 'off')), parts along dimension 0
- right_next: float32 [4, 8192, 256], P('freq', ('off', 'mid')), parts along dimension 0
There are 2 independent parts, one for each index of `freq`. A program takes and returns all parts, laid end to end along the dimension named above; an argument that names none is the same for every part. Nothing has to cross between parts.
All inputs are finite; a program needn't handle non-finite values. No bound on the sum of `trace_mask` on one device may be relied on, other than what follows from the above.
Results may differ from a plain program's by a relative error of at most 0.0011.
Values may be sent and summed in bfloat16 or wider, within the bound.
A program may use at most 192 MiB of HBM per device.

v0:
```python
import math

import jax
import jax.numpy as jnp
from jax import lax
from jax.sharding import PartitionSpec as P

N = 8192


def outer_rows(first, second):
    return jnp.einsum("ik,jk->ij", first, second, preferred_element_type=jnp.float32)


def inner_rows(first, second):
    return jnp.einsum("ij,jk->ik", first, second, preferred_element_type=jnp.float32)


def inner_cols(first, second):
    return jnp.einsum("ij,ik->jk", first, second, preferred_element_type=jnp.float32)


def misfit_of(left_full, right_piece, data_piece, keep_piece):
    real_part = outer_rows(left_full[0], right_piece[0]) + outer_rows(left_full[1], right_piece[1])
    imag_part = outer_rows(left_full[1], right_piece[0]) - outer_rows(left_full[0], right_piece[1])
    miss_re = (keep_piece * (real_part - data_piece[0].astype(jnp.float32))).astype(jnp.bfloat16)
    miss_im = (keep_piece * (imag_part - data_piece[1].astype(jnp.float32))).astype(jnp.bfloat16)
    return (miss_re, miss_im)


def left_terms(miss_re, miss_im, right_piece):
    return jnp.stack(
        [
            inner_rows(miss_re, right_piece[0]) - inner_rows(miss_im, right_piece[1]),
            inner_rows(miss_re, right_piece[1]) + inner_rows(miss_im, right_piece[0]),
        ]
    )


def right_terms(miss_re, miss_im, left_full):
    return jnp.stack(
        [
            inner_cols(miss_re, left_full[0]) + inner_cols(miss_im, left_full[1]),
            inner_cols(miss_re, left_full[1]) - inner_cols(miss_im, left_full[0]),
        ]
    )


def per_device(observed, trace_mask, left_factor, right_factor):
    left_full = lax.all_gather(left_factor, "off", axis=1, tiled=True)
    keep = trace_mask.astype(jnp.float32)
    right_full = lax.all_gather(right_factor, "mid", axis=1, tiled=True)
    miss_re, miss_im = misfit_of(left_full, right_full, observed, keep)
    grad_left = left_terms(miss_re, miss_im, right_full)
    grad_right = right_terms(miss_re, miss_im, left_full)
    right_share = lax.psum_scatter(grad_right, "mid", scatter_dimension=1, tiled=True)
    left_share = lax.psum_scatter(grad_left, "off", scatter_dimension=1, tiled=True)
    step_size = 2.0 / math.sqrt(N)
    left_next = left_factor.astype(jnp.float32) - step_size * left_share
    right_next = right_factor.astype(jnp.float32) - step_size * right_share
    return (left_next, right_next)


def solution(mesh):
    in_specs = (
        P("freq", "mid", "off"),
        P("mid", "off"),
        P("freq", ("mid", "off"), None),
        P("freq", ("off", "mid"), None),
    )
    out_specs = (P("freq", ("mid", "off"), None), P("freq", ("off", "mid"), None))
    return jax.shard_map(
        per_device, mesh=mesh, in_specs=in_specs, out_specs=out_specs, check_vma=False
    )
```

profile of v0, /device:TPU:0, one launch (start us, length us, event | category | flops | bytes accessed | tf_op | source)
XLA Modules:
  0.0 293.8 jit_solution(10524252875861660480)
XLA Ops:
  7.2 0.0 all-gather.3.cloned.1.call-start
  7.2 0.7 all-gather.3.cloned.1.call-update
  7.9 0.0 all-gather.5.cloned.1.call-start
  7.9 0.7 all-gather.5.cloned.1.call-update
  8.6 0.0 reduce-scatter.5.cloned.1.call-start
  8.7 26.2 %all-gather.3.cloned.1.call-done = bf16[2,2048,256]{2,1,0:T(8,128)(2,1)} async-done(((bf16[2,512,256]{2,1,0:T(8,128)(2,1)}), bf16[2,2048,256]{2,1,0:T(8,128)(2,1)}) %all-gather.3.cloned.1.call-update) | async-done | bytes 2097168 | tf_op jit(solution)/shard_map/all_gather | solution.py:50
  34.9 47.5 %all-gather.5.cloned.1.call-done = bf16[2,2048,256]{2,1,0:T(8,128)(2,1)} async-done(((bf16[2,512,256]{2,1,0:T(8,128)(2,1)}), bf16[2,2048,256]{2,1,0:T(8,128)(2,1)}) %all-gather.5.cloned.1.call-update) | async-done | bytes 2097168 | tf_op jit(solution)/shard_map/all_gather | solution.py:52
  82.4 0.0 copy-start.3
  82.4 9.8 %fusion.10 = f32[2048,2048]{1,0:T(8,128)} fusion(bf16[2,2048,256]{2,1,0:T(8,128)(2,1)} %all-gather.5.cloned.1.call-done, bf16[2,2048,256]{2,1,0:T(8,128)(2,1)} %all-gather.3.cloned.1.call-done), kind=kOutput, calls=%fused_computation.24 | convolution fusion | flops 2147483648 | bytes 18874368 | tf_op jit(solution)/shard_map/ik,jk->ij/dot_general | solution.py:12
  92.2 0.0 copy-done.2
  92.2 0.0 copy-done.3
  92.2 8.1 %fusion.9 = f32[2048,2048]{1,0:T(8,128)} fusion(bf16[2,2048,256]{2,1,0:T(8,128)(2,1)S(1)} %copy-done.3, bf16[2,2048,256]{2,1,0:T(8,128)(2,1)S(1)} %copy-done.2), kind=kOutput, calls=%fused_computation.23 | convolution fusion | flops 2147483648 | bytes 18874368 | tf_op jit(solution)/shard_map/ik,jk->ij/dot_general | solution.py:12
  100.4 18.5 %fusion.3 = bf16[2048,2048]{1,0:T(8,128)(2,1)} fusion(f32[2048,2048]{1,0:T(8,128)} %fusion.9, s32[2048,2048]{1,0:T(8,128)} %param.5, bf16[2,2048,2048]{2,1,0:T(8,128)(2,1)} %param.4, bf16[2,2048,256]{2,1,0:T(8,128)(2,1)} %all-gather.3.cloned.1.call-done, bf16[2,2048,256]{2,1,0:T(8,128)(2,1)S(1)} %copy-done.2), kind=kOutput, calls=%fused_computation.5 | convolution fusion | flops 2172649472 | bytes 52428800 | tf_op jit(solution)/shard_map/ik,jk->ij/dot_general | solution.py:12
  118.9 0.0 copy-start.4
  118.9 7.6 %fusion.12 = f32[2048,256]{1,0:T(8,128)} fusion(bf16[2048,2048]{1,0:T(8,128)(2,1)} %fusion.3, bf16[2,2048,256]{2,1,0:T(8,128)(2,1)} %all-gather.3.cloned.1.call-done), kind=kOutput, calls=%fused_computation.26 | convolution fusion | flops 2147483648 | bytes 11534336 | tf_op jit(solution)/shard_map/ij,ik->jk/dot_general | solution.py:20
  126.4 0.0 copy-done.1
  126.4 0.0 copy-done.4
  126.4 4.0 %fusion.8 = f32[2048,256]{1,0:T(8,128)} fusion(bf16[2048,2048]{1,0:T(8,128)(2,1)S(1)} %copy-done.1, bf16[2,2048,256]{2,1,0:T(8,128)(2,1)S(1)} %copy-done.4), kind=kOutput, calls=%fused_computation.22 | convolution fusion | flops 2147483648 | bytes 11534336 | tf_op jit(solution)/shard_map/ij,ik->jk/dot_general | solution.py:20
  130.5 18.6 %fusion.1 = bf16[2048,2048]{1,0:T(8,128)(2,1)} fusion(f32[2048,2048]{1,0:T(8,128)} %fusion.10, s32[2048,2048]{1,0:T(8,128)} %param.5, bf16[2,2048,2048]{2,1,0:T(8,128)(2,1)} %param.4, bf16[2,2048,256]{2,1,0:T(8,128)(2,1)} %all-gather.3.cloned.1.call-done, bf16[2,2048,256]{2,1,0:T(8,128)(2,1)S(1)} %copy-done.2), kind=kOutput, calls=%fused_computation.2 | convolution fusion | flops 2172649472 | bytes 52428800 | tf_op jit(solution)/shard_map/ik,jk->ij/dot_general | solution.py:12
  149.0 0.0 copy-start
  149.0 0.0 copy-start.5
  149.0 0.0 copy-start.8
  149.0 7.0 %fusion.4 = f32[1,2048,256]{2,1,0:T(8,128)S(1)} fusion(f32[2048,256]{1,0:T(8,128)} %fusion.12, bf16[2048,2048]{1,0:T(8,128)(2,1)} %fusion.1, bf16[2,2048,256]{2,1,0:T(8,128)(2,1)} %all-gather.3.cloned.1.call-done), kind=kOutput, calls=%fused_computation.9 | convolution fusion | flops 2148007936 | bytes 13631488 | tf_op jit(solution)/shard_map/ij,ik->jk/dot_general | solution.py:20
  156.0 0.0 copy-done
  156.1 0.3 copy-done.5
  156.3 0.6 copy-done.8
  156.9 2.5 fusion.5
  159.5 2.2 pad_maximum_fusion.1
  161.7 0.0 reduce-scatter.5.cloned.1.call-update
  161.7 0.3 reduce-scatter.3.cloned.1.call-start
  162.0 0.0 slice-start
  162.1 5.9 %fusion.13 = f32[2048,256]{1,0:T(8,128)S(1)} fusion(bf16[2048,2048]{1,0:T(8,128)(2,1)} %fusion.3, bf16[2,2048,256]{2,1,0:T(8,128)(2,1)S(1)} %copy-done.2), kind=kOutput, calls=%fused_computation.27 | convolution fusion | flops 2147483648 | bytes 11534336 | tf_op jit(solution)/shard_map/ij,jk->ik/dot_general | solution.py:16
  167.9 0.0 slice-start.1
  168.0 5.9 %fusion.11 = f32[2048,256]{1,0:T(8,128)S(1)} fusion(bf16[2048,2048]{1,0:T(8,128)(2,1)} %fusion.3, bf16[2,2048,256]{2,1,0:T(8,128)(2,1)S(1)} %copy-done.2), kind=kOutput, calls=%fused_computation.25 | convolution fusion | flops 2147483648 | bytes 11534336 | tf_op jit(solution)/shard_map/ij,jk->ik/dot_general | solution.py:16
  173.8 0.0 slice-done
  173.9 0.0 slice-done.1
  173.9 2.4 fusion.7
  176.2 2.4 fusion.6
  178.6 2.2 pad_maximum_fusion
  180.8 0.0 copy-start.6
  180.8 0.0 copy-start.7
  180.8 0.0 reduce-scatter.3.cloned.1.call-update
  180.9 56.5 %reduce-scatter.5.cloned.1.call-done = f32[2,512,256]{2,1,0:T(8,128)} async-done(((f32[2,2048,256]{2,1,0:T(8,128)}), f32[2,512,256]{2,1,0:T(8,128)}) %reduce-scatter.5.cloned.1.call-update) | async-done | bytes 1048592 | tf_op jit(solution)/shard_map/reduce_scatter | solution.py:56
  237.4 0.0 copy-done.6
  237.4 2.3 multiply_subtract_fusion
  239.7 45.3 %reduce-scatter.3.cloned.1.call-done = f32[2,512,256]{2,1,0:T(8,128)} async-done(((f32[2,2048,256]{2,1,0:T(8,128)}), f32[2,512,256]{2,1,0:T(8,128)}) %reduce-scatter.3.cloned.1.call-update) | async-done | bytes 1048592 | tf_op jit(solution)/shard_map/reduce_scatter | solution.py:57
  285.0 0.0 copy-done.7
  285.0 2.3 multiply_subtract_fusion.1
  (3 shorter events, 0.0 us)
Async XLA Ops:
  7.2 27.7 %all-gather.3.cloned.1.call-start = ((), (), s32[]{:S(2)}) async-start(), calls=%async_computation.2 | async-start | bytes 2621440 | tf_op jit(solution)/shard_map/all_gather | solution.py:50
  7.9 74.5 %all-gather.5.cloned.1.call-start = ((), (), s32[]{:S(2)}) async-start(), calls=%async_computation.3 | async-start | bytes 2621440 | tf_op jit(solution)/shard_map/all_gather | solution.py:52
  8.6 228.7 %reduce-scatter.5.cloned.1.call-start = ((), (), s32[]{:S(2)}) async-start(), calls=%async_computation.5 | async-start | bytes 5242880 | tf_op jit(solution)/shard_map/reduce_scatter | solution.py:56
  82.4 9.8 %copy-start.2 = (bf16[2,2048,256]{2,1,0:T(8,128)(2,1)S(1)}, bf16[2,2048,256]{2,1,0:T(8,128)(2,1)}, u32[]{:S(2)}) copy-start(bf16[2,2048,256]{2,1,0:T(8,128)(2,1)} %all-gather.5.cloned.1.call-done) | copy-start | bytes 6291460
  82.4 9.8 %copy-start.3 = (bf16[2,2048,256]{2,1,0:T(8,128)(2,1)S(1)}, bf16[2,2048,256]{2,1,0:T(8,128)(2,1)}, u32[]{:S(2)}) copy-start(bf16[2,2048,256]{2,1,0:T(8,128)(2,1)} %all-gather.3.cloned.1.call-done) | copy-start | bytes 6291460
  118.9 7.6 %copy-start.1 = (bf16[2048,2048]{1,0:T(8,128)(2,1)S(1)}, bf16[2048,2048]{1,0:T(8,128)(2,1)}, u32[]{:S(2)}) copy-start(bf16[2048,2048]{1,0:T(8,128)(2,1)} %fusion.3) | copy-start | bytes 25165828
  118.9 7.6 %copy-start.4 = (bf16[2,2048,256]{2,1,0:T(8,128)(2,1)S(1)}, bf16[2,2048,256]{2,1,0:T(8,128)(2,1)}, u32[]{:S(2)}) copy-start(bf16[2,2048,256]{2,1,0:T(8,128)(2,1)} %all-gather.3.cloned.1.call-done) | copy-start | bytes 6291460
  149.0 7.0 %copy-start = (bf16[2048,2048]{1,0:T(8,128)(2,1)S(1)}, bf16[2048,2048]{1,0:T(8,128)(2,1)}, u32[]{:S(2)}) copy-start(bf16[2048,2048]{1,0:T(8,128)(2,1)} %fusion.1) | copy-start | bytes 25165828
  149.0 7.3 %copy-start.5 = (bf16[2,2048,256]{2,1,0:T(8,128)(2,1)S(1)}, bf16[2,2048,256]{2,1,0:T(8,128)(2,1)}, u32[]{:S(2)}) copy-start(bf16[2,2048,256]{2,1,0:T(8,128)(2,1)} %all-gather.3.cloned.1.call-done) | copy-start | bytes 6291460
  149.0 7.9 %copy-start.8 = (f32[2048,256]{1,0:T(8,128)S(1)}, f32[2048,256]{1,0:T(8,128)}, u32[]{:S(2)}) copy-start(f32[2048,256]{1,0:T(8,128)} %fusion.8) | copy-start | bytes 6291460
  161.7 123.2 %reduce-scatter.3.cloned.1.call-start = ((), (), s32[]{:S(2)}) async-start(), calls=%async_computation.4 | async-start | bytes 5242880 | tf_op jit(solution)/shard_map/reduce_scatter | solution.py:57
  162.0 11.8 %slice-start = ((s8[8388608]{0:T(1024)(128)(4,1)}), s8[4194304]{0:T(1024)(128)(4,1)S(1)}, s32[]{:S(2)}) async-start(s8[8388608]{0:T(1024)(128)(4,1)} %bitcast.46), calls=%async_computation.6 | async-start | bytes 8388608
  167.9 5.9 %slice-start.1 = ((s8[8388608]{0:T(1024)(128)(4,1)}), s8[4194304]{0:T(1024)(128)(4,1)S(1)}, s32[]{:S(2)}) async-start(s8[8388608]{0:T(1024)(128)(4,1)} %bitcast.46), calls=%async_computation.7 | async-start | bytes 8388608
  180.8 56.5 %copy-start.6 = (bf16[2,512,256]{2,1,0:T(8,128)(2,1)S(1)}, bf16[2,512,256]{2,1,0:T(8,128)(2,1)}, u32[]{:S(2)}) copy-start(bf16[2,512,256]{2,1,0:T(8,128)(2,1)} %param.7) | copy-start | bytes 1572868
  180.8 104.1 %copy-start.7 = (bf16[2,512,256]{2,1,0:T(8,128)(2,1)S(1)}, bf16[2,512,256]{2,1,0:T(8,128)(2,1)}, u32[]{:S(2)}) copy-start(bf16[2,512,256]{2,1,0:T(8,128)(2,1)} %param.6) | copy-start | bytes 1572868
Sparse Core Ops, SparseCore 0:
  9.6 25.2 all-gather.2
  36.4 45.9 all-gather.4
  161.9 75.4 reduce-scatter.4
  239.9 45.0 reduce-scatter.2
where the time goes:
time: 294 us
  waiting for transfers between devices  177 us (60%)
  matrix products  92.6 us (31%)
  between operations  13.9 us (5%)
  other arithmetic  9.1 us (3%)
    reduce_scatter x1, waiting for transfers between devices, per_device(): lax.psum_scatter(grad_right, 'mid', scatter_dimension=1, tiled=True)  56.5 us
    dot_general x4, matrix products, outer_rows(): jnp.einsum('ik,jk->ij', first, second, preferred_element_type=jnp.float32)  55 us
    all_gather x1, waiting for transfers between devices, per_device(): right_full = lax.all_gather(right_factor, 'mid', axis=1, tiled=True)  47.5 us
    reduce_scatter x1, waiting for transfers between devices, per_device(): lax.psum_scatter(grad_left, 'off', scatter_dimension=1, tiled=True)  45.3 us
    all_gather x1, waiting for transfers between devices, per_device(): left_full = lax.all_gather(left_factor, 'off', axis=1, tiled=True)  26.2 us
    dot_general x4, matrix products, inner_cols(): jnp.einsum('ij,ik->jk', first, second, preferred_element_type=jnp.float32)  21.2 us
    dot_general x4, matrix products, inner_rows(): jnp.einsum('ij,jk->ik', first, second, preferred_element_type=jnp.float32)  16.5 us
  transfers between devices with their start and end apart: 4, of which 4 were waited for; matrix products, arithmetic and copies ran while one was open for 7% of the time, Pallas kernels for 0%

commit v1 on v0

v1 whole, which is shorter than its diff:
```python
import math

import jax
import jax.numpy as jnp
from jax import lax
from jax.experimental import pallas as pl
from jax.experimental.pallas import tpu as pltpu
from jax.sharding import PartitionSpec as P

N = 8192
STEP = 2.0 / math.sqrt(N)
LINK = jnp.int16
LEVELS = 32000.0
PIECES = 4
MESH = pl.DeviceIdType.MESH


def outer_rows(first, second):
    return jnp.einsum("ik,jk->ij", first, second, preferred_element_type=jnp.float32)


def inner_rows(first, second):
    return jnp.einsum("ij,jk->ik", first, second, preferred_element_type=jnp.float32)


def inner_cols(first, second):
    return jnp.einsum("ij,ik->jk", first, second, preferred_element_type=jnp.float32)


def plain_device(observed, trace_mask, left_factor, right_factor):
    left = lax.all_gather(left_factor, "off", axis=1, tiled=True)
    keep = trace_mask.astype(jnp.float32)
    right = lax.all_gather(right_factor, "mid", axis=1, tiled=True)
    real_part = outer_rows(left[0], right[0]) + outer_rows(left[1], right[1])
    imag_part = outer_rows(left[1], right[0]) - outer_rows(left[0], right[1])
    miss_re = (keep * (real_part - observed[0].astype(jnp.float32))).astype(jnp.bfloat16)
    miss_im = (keep * (imag_part - observed[1].astype(jnp.float32))).astype(jnp.bfloat16)
    grad_left = jnp.stack(
        [
            inner_rows(miss_re, right[0]) - inner_rows(miss_im, right[1]),
            inner_rows(miss_re, right[1]) + inner_rows(miss_im, right[0]),
        ]
    )
    grad_right = jnp.stack(
        [
            inner_cols(miss_re, left[0]) + inner_cols(miss_im, left[1]),
            inner_cols(miss_re, left[1]) - inner_cols(miss_im, left[0]),
        ]
    )
    right_share = lax.psum_scatter(grad_right, "mid", scatter_dimension=1, tiled=True)
    left_share = lax.psum_scatter(grad_left, "off", scatter_dimension=1, tiled=True)
    left_next = left_factor.astype(jnp.float32) - STEP * left_share
    right_next = right_factor.astype(jnp.float32) - STEP * right_share
    return (left_next, right_next)


def coded(value):
    top = jnp.maximum(jnp.max(jnp.abs(value), axis=0, keepdims=True), 1e-30)
    levels = jnp.floor(value * (LEVELS / top) + 0.5)
    return levels.astype(jnp.int32).astype(LINK), top * (1.0 / LEVELS)


class Both:
    def __init__(self, *copies):
        self.copies = copies

    def start(self):
        for c in self.copies:
            c.start()

    def wait_recv(self):
        for c in self.copies:
            c.wait_recv()

    def wait_send(self):
        for c in self.copies:
            c.wait_send()


def kernel(
    n, rb, k, tr,
    obs_hbm, mask_hbm, left_hbm, right_hbm,
    gl_out, gr_out,
    lfull, rcat, rbig, lt, obs, mask, gl, gr,
    zsend, zrecv, asend, arecv, bsend, brecv,
    zsend_s, zrecv_s, asend_s, arecv_s, bsend_s, brecv_s,
    in_sem, obs_sem, mask_sem,
    g_send_r, g_send_l, g_recv,
    l_send, l_recv,
    z_send_sem, z_recv_sem,
    a_send_sem, a_recv_sem, b_send_sem, b_recv_sem,
    z_send_sem_s, z_recv_sem_s, a_send_sem_s, a_recv_sem_s, b_send_sem_s, b_recv_sem_s,
):
    me = lax.axis_index("mid")
    off = lax.axis_index("off")
    sib = off + 1 - 2 * lax.rem(off, 2)
    cross = lax.rem(off + 2, 4)
    diag = lax.rem(sib + 2, 4)
    lo = jnp.minimum(me, n - 1 - me)
    has_l = me > 0
    has_r = me < n - 1
    piece = 2 * k // PIECES
    tiles = rb // tr

    def block_at(j):
        near = (j + 1) // 2
        up = lax.rem(j, 2) == 1
        paired = jnp.where(up, me + near, me - near)
        far = j - lo
        single = jnp.where(me < n - 1 - me, me + far, me - far)
        return jnp.where(j <= 2 * lo, paired, single)

    def row_block(q):
        return jnp.where(q == 0, off, jnp.where(q == 1, sib, jnp.where(q == 2, cross, diag)))

    def obs_copy(j):
        b = block_at(j)
        cols = pl.ds(pl.multiple_of(b * rb, rb), rb)
        slot = lax.rem(j, 2)
        return (
            pltpu.make_async_copy(obs_hbm.at[:, :, cols], obs.at[slot], obs_sem.at[slot]),
            pltpu.make_async_copy(mask_hbm.at[:, cols], mask.at[slot], mask_sem.at[slot]),
        )

    def gather_right(b):
        return pltpu.make_async_remote_copy(
            src_ref=rcat.at[b], dst_ref=rcat.at[b], send_sem=g_send_r.at[b], recv_sem=g_recv.at[b],
            device_id={"mid": jnp.minimum(me + 1, n - 1)}, device_id_type=MESH)

    def gather_left(b):
        return pltpu.make_async_remote_copy(
            src_ref=rcat.at[b], dst_ref=rcat.at[b], send_sem=g_send_l.at[b], recv_sem=g_recv.at[b],
            device_id={"mid": jnp.maximum(me - 1, 0)}, device_id_type=MESH)

    def left_copy(block, to, which):
        return pltpu.make_async_remote_copy(
            src_ref=lfull.at[block], dst_ref=lfull.at[block],
            send_sem=l_send.at[which], recv_sem=l_recv.at[which],
            device_id={"off": to}, device_id_type=MESH)

    def arrive(b):
        @pl.when(b < me)
        def _():
            gather_right(b).wait_recv()

            @pl.when(has_r)
            def _():
                gather_right(b).start()

        @pl.when(b > me)
        def _():
            gather_left(b).wait_recv()

            @pl.when(has_l)
            def _():
                gather_left(b).start()

    def sum_right(t, p):
        to = jnp.minimum(me + 1, n - 1)
        return Both(
            pltpu.make_async_remote_copy(
                src_ref=zsend.at[t, p], dst_ref=zrecv.at[t, p],
                send_sem=z_send_sem.at[t, p], recv_sem=z_recv_sem.at[t, p],
                device_id={"mid": to}, device_id_type=MESH),
            pltpu.make_async_remote_copy(
                src_ref=zsend_s.at[t, p], dst_ref=zrecv_s.at[t, p],
                send_sem=z_send_sem_s.at[t, p], recv_sem=z_recv_sem_s.at[t, p],
                device_id={"mid": to}, device_id_type=MESH))

    def sum_left(t, p):
        to = jnp.maximum(me - 1, 0)
        slot = jnp.where(t == me - 1, n, t)
        return Both(
            pltpu.make_async_remote_copy(
                src_ref=zsend.at[t, p], dst_ref=zrecv.at[slot, p],
                send_sem=z_send_sem.at[t, p], recv_sem=z_recv_sem.at[slot, p],
                device_id={"mid": to}, device_id_type=MESH),
            pltpu.make_async_remote_copy(
                src_ref=zsend_s.at[t, p], dst_ref=zrecv_s.at[slot, p],
                send_sem=z_send_sem_s.at[t, p], recv_sem=z_recv_sem_s.at[slot, p],
                device_id={"mid": to}, device_id_type=MESH))

    def sum_arrived(slot, p):
        return Both(
            pltpu.make_async_remote_copy(
                src_ref=zrecv.at[slot, p], dst_ref=zrecv.at[slot, p],
                send_sem=z_send_sem.at[0, p], recv_sem=z_recv_sem.at[slot, p],
                device_id={"off": sib}, device_id_type=MESH),
            pltpu.make_async_remote_copy(
                src_ref=zrecv_s.at[slot, p], dst_ref=zrecv_s.at[slot, p],
                send_sem=z_send_sem_s.at[0, p], recv_sem=z_recv_sem_s.at[slot, p],
                device_id={"off": sib}, device_id_type=MESH))

    def a_copy(which):
        return Both(
            pltpu.make_async_remote_copy(
                src_ref=asend.at[which], dst_ref=arecv.at[which],
                send_sem=a_send_sem.at[which], recv_sem=a_recv_sem.at[which],
                device_id={"off": sib}, device_id_type=MESH),
            pltpu.make_async_remote_copy(
                src_ref=asend_s.at[which], dst_ref=arecv_s.at[which],
                send_sem=a_send_sem_s.at[which], recv_sem=a_recv_sem_s.at[which],
                device_id={"off": sib}, device_id_type=MESH))

    def b_copy():
        return Both(
            pltpu.make_async_remote_copy(
                src_ref=bsend, dst_ref=brecv, send_sem=b_send_sem, recv_sem=b_recv_sem,
                device_id={"off": cross}, device_id_type=MESH),
            pltpu.make_async_remote_copy(
                src_ref=bsend_s, dst_ref=brecv_s, send_sem=b_send_sem_s, recv_sem=b_recv_sem_s,
                device_id={"off": cross}, device_id_type=MESH))

    def z_received(slot, p):
        return zrecv[slot, p].astype(jnp.float32) * zrecv_s[slot, p]

    def z_put(t, p, value):
        zsend[t, p], zsend_s[t, p] = coded(value)

    own = [
        pltpu.make_async_copy(left_hbm.at[0], lfull.at[off, :, 0:k], in_sem.at[0]),
        pltpu.make_async_copy(left_hbm.at[1], lfull.at[off, :, k:2 * k], in_sem.at[1]),
        pltpu.make_async_copy(right_hbm.at[0], rcat.at[me, :, 0:k], in_sem.at[2]),
        pltpu.make_async_copy(right_hbm.at[1], rcat.at[me, :, k:2 * k], in_sem.at[3]),
    ]
    for c in own:
        c.start()
    for c in obs_copy(0):
        c.start()

    barrier = pltpu.get_barrier_semaphore()
    for to in (sib, cross):
        pl.semaphore_signal(barrier, inc=1, device_id={"off": to}, device_id_type=MESH)

    @pl.when(has_l)
    def _():
        pl.semaphore_signal(barrier, inc=1, device_id={"mid": me - 1}, device_id_type=MESH)

    @pl.when(has_r)
    def _():
        pl.semaphore_signal(barrier, inc=1, device_id={"mid": me + 1}, device_id_type=MESH)

    pl.semaphore_wait(barrier, 2 + jnp.where(has_l, 1, 0) + jnp.where(has_r, 1, 0))

    for c in own:
        c.wait()

    left_copy(off, cross, 1).start()
    left_copy(off, sib, 0).start()

    @pl.when(has_r)
    def _():
        gather_right(me).start()

    @pl.when(has_l)
    def _():
        gather_left(me).start()

    gl[...] = jnp.zeros_like(gl)

    def step(j, carry):
        b = block_at(j)
        slot = lax.rem(j, 2)

        @pl.when(j < n - 1)
        def _():
            for c in obs_copy(j + 1):
                c.start()

        rbig[0:rb, :] = rcat[b]
        rbig[rb:2 * rb, 0:k] = -rcat[b, :, k:2 * k]
        rbig[rb:2 * rb, k:2 * k] = rcat[b, :, 0:k]
        gr[b] = jnp.zeros(gr.shape[1:], jnp.float32)
        for c in obs_copy(j):
            c.wait()

        def rows(i, carry):
            q_of = i // tiles
            t = lax.rem(i, tiles)
            q = jnp.where(j == n - 1, 3 - q_of, q_of)
            block = row_block(q)

            @pl.when(jnp.logical_and(j == 0, t == 0))
            def _():
                @pl.when(q == 1)
                def _():
                    left_copy(sib, sib, 0).wait_recv()

                @pl.when(q == 2)
                def _():
                    left_copy(cross, cross, 1).wait_recv()
                    left_copy(cross, sib, 2).start()

                @pl.when(q == 3)
                def _():
                    left_copy(diag, sib, 2).wait_recv()

            @pl.when(jnp.logical_and(j < n - 1, i == 2 * tiles))
            def _():
                nxt = j + 1
                pair = jnp.logical_and(nxt <= 2 * lo, lax.rem(nxt, 2) == 1)

                @pl.when(pair)
                def _():
                    near = (nxt + 1) // 2
                    arrive(me + near)
                    arrive(me - near)

                @pl.when(nxt > 2 * lo)
                def _():
                    arrive(block_at(nxt))

            at = pl.ds(pl.multiple_of(t * tr, tr), tr)
            row_at = pl.ds(pl.multiple_of(block * rb + t * tr, tr), tr)
            lrows = lfull[block, at, :]

            @pl.when(j == 0)
            def _():
                turned = lrows.astype(jnp.float32).T.astype(jnp.bfloat16)
                lt[block * tiles + t, :, 0:tr] = turned
                lt[block * tiles + t, 0:k, tr:2 * tr] = turned[k:2 * k]
                lt[block * tiles + t, k:2 * k, tr:2 * tr] = -turned[0:k]

            pred = lax.dot_general(
                lrows, rbig[...], (((1,), (1,)), ((), ())), preferred_element_type=jnp.float32)
            keep = mask[slot, row_at, :] != 0
            miss_re = jnp.where(
                keep, pred[:, 0:rb] - obs[slot, 0, row_at, :].astype(jnp.float32), 0.0
            ).astype(jnp.bfloat16)
            miss_im = jnp.where(
                keep, pred[:, rb:2 * rb] - obs[slot, 1, row_at, :].astype(jnp.float32), 0.0
            ).astype(jnp.bfloat16)
            gl[block, at, :] += jnp.dot(
                jnp.concatenate([miss_re, miss_im], axis=1), rbig[...],
                preferred_element_type=jnp.float32)
            gr[b] += jnp.dot(
                lt[block * tiles + t], jnp.concatenate([miss_re, miss_im], axis=0),
                preferred_element_type=jnp.float32)

            @pl.when(jnp.logical_and(j == n - 1, t == tiles - 1))
            def _():
                @pl.when(q == 3)
                def _():
                    asend[0], asend_s[0] = coded(gl[diag])
                    a_copy(0).start()

                @pl.when(q == 1)
                def _():
                    asend[1], asend_s[1] = coded(gl[sib])
                    a_copy(1).start()

            return carry

        lax.fori_loop(0, 4 * tiles, rows, 0)

        @pl.when(jnp.logical_and(me == 0, b > me))
        def _():
            for p in range(PIECES):
                z_put(b, p, gr[b, p * piece:(p + 1) * piece, :])
                sum_right(b, p).start()

        @pl.when(jnp.logical_and(me == n - 1, b < me))
        def _():
            for p in range(PIECES):
                z_put(b, p, gr[b, p * piece:(p + 1) * piece, :])
                sum_left(b, p).start()

        return carry

    lax.fori_loop(0, n, step, 0)

    a_copy(0).wait_recv()
    bsend[...], bsend_s[...] = coded(gl[cross] + arecv[0].astype(jnp.float32) * arecv_s[0])
    b_copy().start()

    def pass_on(tau, carry):
        right_t = tau - me
        left_t = 2 * (n - 1) - me - tau

        @pl.when((me > 0) & (right_t > me) & (right_t < n))
        def _():
            for p in range(PIECES):
                sum_arrived(right_t, p).wait_recv()
                z_put(right_t, p, gr[right_t, p * piece:(p + 1) * piece, :] + z_received(right_t, p))
                sum_right(right_t, p).start()

        @pl.when((me < n - 1) & (left_t < me) & (left_t >= 0))
        def _():
            for p in range(PIECES):
                sum_arrived(left_t, p).wait_recv()
                z_put(left_t, p, gr[left_t, p * piece:(p + 1) * piece, :] + z_received(left_t, p))
                sum_left(left_t, p).start()

        return carry

    lax.fori_loop(0, 2 * n, pass_on, 0)

    a_copy(1).wait_recv()
    gl_out[...] = gl[off] + arecv[1].astype(jnp.float32) * arecv_s[1]
    b_copy().wait_recv()
    gl_out[...] += brecv[...].astype(jnp.float32) * brecv_s[...]

    for p in range(PIECES):
        span = slice(p * piece, (p + 1) * piece)

        @pl.when(has_l)
        def _(p=p, span=span):
            sum_arrived(me, p).wait_recv()
            gr[me, span, :] += z_received(me, p)

        @pl.when(has_r)
        def _(p=p, span=span):
            sum_arrived(n, p).wait_recv()
            gr[me, span, :] += z_received(n, p)

        gr_out[:, span] = gr[me, span, :].T

    left_copy(off, cross, 1).wait_send()
    left_copy(off, sib, 0).wait_send()
    left_copy(cross, sib, 2).wait_send()
    for which in range(2):
        a_copy(which).wait_send()
    b_copy().wait_send()

    def drain(t, carry):
        @pl.when(has_r & (t <= me))
        def _():
            gather_right(t).wait_send()

        @pl.when(has_l & (t >= me))
        def _():
            gather_left(t).wait_send()

        @pl.when(t > me)
        def _():
            for p in range(PIECES):
                sum_right(t, p).wait_send()

        @pl.when(t < me)
        def _():
            for p in range(PIECES):
                sum_left(t, p).wait_send()

        return carry

    lax.fori_loop(0, n, drain, 0)


def kernel_device(n, observed, trace_mask, left_factor, right_factor):
    rb, k = left_factor.shape[1:]
    n_off = 4
    rows = rb * n_off
    tr = min(256, rb)
    tiles = rows // tr
    dma = pltpu.SemaphoreType.DMA
    any_spec = pl.BlockSpec(memory_space=pl.ANY)
    vmem_spec = pl.BlockSpec(memory_space=pltpu.VMEM)
    bf16, f32 = jnp.bfloat16, jnp.float32
    left_share, right_share = pl.pallas_call(
        lambda *refs: kernel(n, rb, k, tr, *refs),
        out_shape=[
            jax.ShapeDtypeStruct((rb, 2 * k), f32),
            jax.ShapeDtypeStruct((rb, 2 * k), f32),
        ],
        in_specs=[any_spec] * 4,
        out_specs=[vmem_spec] * 2,
        scratch_shapes=[
            pltpu.VMEM((n_off, rb, 2 * k), bf16),
            pltpu.VMEM((n, rb, 2 * k), bf16),
            pltpu.VMEM((2 * rb, 2 * k), bf16),
            pltpu.VMEM((tiles, 2 * k, 2 * tr), bf16),
            pltpu.VMEM((2, 2, rows, rb), bf16),
            pltpu.VMEM((2, rows, rb), jnp.int32),
            pltpu.VMEM((n_off, rb, 2 * k), f32),
            pltpu.VMEM((n, 2 * k, rb), f32),
            pltpu.VMEM((n, PIECES, 2 * k // PIECES, rb), LINK),
            pltpu.VMEM((n + 1, PIECES, 2 * k // PIECES, rb), LINK),
            pltpu.VMEM((2, rb, 2 * k), LINK),
            pltpu.VMEM((2, rb, 2 * k), LINK),
            pltpu.VMEM((rb, 2 * k), LINK),
            pltpu.VMEM((rb, 2 * k), LINK),
            pltpu.VMEM((n, PIECES, 1, rb), f32),
            pltpu.VMEM((n + 1, PIECES, 1, rb), f32),
            pltpu.VMEM((2, 1, 2 * k), f32),
            pltpu.VMEM((2, 1, 2 * k), f32),
            pltpu.VMEM((1, 2 * k), f32),
            pltpu.VMEM((1, 2 * k), f32),
            dma((4,)), dma((2,)), dma((2,)),
            dma((n,)), dma((n,)), dma((n,)),
            dma((3,)), dma((3,)),
            dma((n, PIECES)), dma((n + 1, PIECES)),
            dma((2,)), dma((2,)), dma(()), dma(()),
            dma((n, PIECES)), dma((n + 1, PIECES)),
            dma((2,)), dma((2,)), dma(()), dma(()),
        ],
        compiler_params=pltpu.CompilerParams(
            collective_id=0, has_side_effects=True, vmem_limit_bytes=60 * 1024 * 1024),
        cost_estimate=pl.CostEstimate(
            flops=24 * rows * n * rb * k, bytes_accessed=8 * rows * n * rb, transcendentals=0),
    )(observed, trace_mask, left_factor, right_factor)
    left_share = jnp.stack([left_share[:, :k], left_share[:, k:]])
    right_share = jnp.stack([right_share[:, :k], right_share[:, k:]])
    left_next = left_factor.astype(f32) - STEP * left_share
    right_next = right_factor.astype(f32) - STEP * right_share
    return (left_next, right_next)


def solution(mesh):
    n, n_off = mesh.shape["mid"], mesh.shape["off"]

    def per_device(observed, trace_mask, left_factor, right_factor):
        rb, k = left_factor.shape[1:]
        if n_off == 4 and 2 <= n <= 4 and rb % 256 == 0 and rb <= 512 and k == 256:
            return kernel_device(n, observed, trace_mask, left_factor, right_factor)
        return plain_device(observed, trace_mask, left_factor, right_factor)

    in_specs = (
        P("freq", "mid", "off"),
        P("mid", "off"),
        P("freq", ("mid", "off"), None),
        P("freq", ("off", "mid"), None),
    )
    out_specs = (P("freq", ("mid", "off"), None), P("freq", ("off", "mid"), None))
    return jax.shard_map(
        per_device, mesh=mesh, in_specs=in_specs, out_specs=out_specs, check_vma=False
    )
```

time: 294 us -> 94.8 us (0.32)
  waiting for transfers between devices: 177 us -> 0 us
  matrix products: 92.6 us -> 0 us
  Pallas kernels: 0 us -> 90.1 us
  between operations: 13.9 us -> 0.67 us
  other arithmetic: 9.1 us -> 2.23 us
    reduce_scatter x2 -> x0, waiting for transfers between devices: 102 us -> none  [the longest x1 56.5 us: per_device(): lax.psum_scatter(grad_right, 'mid', scatter_dimension=1, tiled=True)]
    dot_general x12 -> x0, matrix products: 92.6 us -> none  [the longest x4 55 us: outer_rows(): jnp.einsum('ik,jk->ij', first, second, preferred_element_type=jnp.float32)]
    pallas_call x0 -> x1, Pallas kernels: none -> 90.1 us  [kernel_device(): pl.pallas_call(lambda *refs: kernel(n, rb, k, tr, *refs), out_shape=[jax....]
    all_gather x2 -> x0, waiting for transfers between devices: 73.7 us -> none  [the longest x1 47.5 us: per_device(): right_full = lax.all_gather(right_factor, 'mid', axis=1, tiled=True)]
    another operation x2 -> x0, other arithmetic: 4.47 us -> none  [the longest x1 2.25 us: right_terms(): jnp.stack([inner_cols(miss_re, left_full[0]) + inner_cols(miss_im, left_f...]
  transfers between devices with their start and end apart: 4 -> 0, of which waited for: 4 -> 0; matrix products, arithmetic and copies ran while one was open for 7% -> 0% of each run, Pallas kernels for 0% -> 0%
where the time goes in v1:
time: 94.8 us; the launch traced here: 94.6 us
  Pallas kernels  90.1 us (95%)
  other arithmetic  2.23 us (2%)
  local copies, waits for them, and re-layouts  1.66 us (2%)
    pallas_call x1, Pallas kernels, kernel_device(): pl.pallas_call(lambda *refs: kernel(n, rb, k, tr, *refs), out_shape=[jax....  90.1 us

profile of v1, /device:TPU:0, one launch (start us, length us, event | category | flops | bytes accessed | tf_op | source)
XLA Modules:
  0.0 94.6 jit_solution(17361504725859272345)
XLA Ops:
  0.6 0.0 copy-start
  0.6 0.0 copy-start.1
  0.7 90.1 %shard_map.59 = (f32[512,512]{1,0:T(8,128)}, f32[512,512]{1,0:T(8,128)}) custom-call(bf16[2,2048,2048]{2,1,0:T(8,128)(2,1)} %refs_0_.1, s32[2048,2048]{1,0:T(8,128)} %refs_1_.1, bf16[2,512,256]{2,1,0:T(8,128)(2,1)} %refs_2_.1, bf16[2,512,256]{2,1,0:T(8,128)(2,1)} %refs_3_.1), custom_call_target="tpu_custom_call" | custom-call | flops 25769803776 | bytes 33554432 | tf_op jit(solution)/shard_map/pallas_call | solution.py:459
  90.7 1.7 %slice_bitcast_fusion.1 = (f32[1,512,256]{2,1,0:T(8,128)S(1)}, f32[1,512,256]{2,1,0:T(8,128)S(1)}, f32[1,512,256]{2,1,0:T(8,128)S(1)}, f32[1,512,256]{2,1,0:T(8,128)S(1)}) fusion(f32[512,512]{1,0:T(8,128)} %get-tuple-element.5, f32[512,512]{1,0:T(8,128)} %get-tuple-element.4), kind=kLoop, calls=%fused_computation.5 | loop fusion | bytes 4194304 | tf_op jit(solution)/shard_map/stack | solution.py:502
  92.4 0.0 copy-done
  92.4 1.1 %fusion.1 = f32[2,512,256]{2,1,0:T(8,128)} fusion(f32[1,512,256]{2,1,0:T(8,128)S(1)} %get-tuple-element.7, f32[1,512,256]{2,1,0:T(8,128)S(1)} %get-tuple-element.6, bf16[2,512,256]{2,1,0:T(8,128)(2,1)S(1)} %copy-done), kind=kLoop, calls=%fused_computation.3 | loop fusion | flops 1048576 | bytes 2621440 | tf_op jit(solution)/shard_map/sub | solution.py:504
  93.5 0.0 copy-done.1
  93.5 1.1 %fusion = f32[2,512,256]{2,1,0:T(8,128)} fusion(f32[1,512,256]{2,1,0:T(8,128)S(1)} %get-tuple-element.10, f32[1,512,256]{2,1,0:T(8,128)S(1)} %get-tuple-element.11, bf16[2,512,256]{2,1,0:T(8,128)(2,1)S(1)} %copy-done.1), kind=kLoop, calls=%fused_computation.1 | loop fusion | flops 1048576 | bytes 2621440 | tf_op jit(solution)/shard_map/sub | solution.py:503
Async XLA Ops:
  0.6 91.8 %copy-start = (bf16[2,512,256]{2,1,0:T(8,128)(2,1)S(1)}, bf16[2,512,256]{2,1,0:T(8,128)(2,1)}, u32[]{:S(2)}) copy-start(bf16[2,512,256]{2,1,0:T(8,128)(2,1)} %refs_3_.1) | copy-start | bytes 1572868
  0.6 92.9 %copy-start.1 = (bf16[2,512,256]{2,1,0:T(8,128)(2,1)S(1)}, bf16[2,512,256]{2,1,0:T(8,128)(2,1)}, u32[]{:S(2)}) copy-start(bf16[2,512,256]{2,1,0:T(8,128)(2,1)} %refs_2_.1) | copy-start | bytes 1572868

commit v2 on v1

--- a/solution.py
+++ b/solution.py
@@ -11,7 +11,7 @@
 STEP = 2.0 / math.sqrt(N)
 LINK = jnp.int16
 LEVELS = 32000.0
-PIECES = 4
+PIECES = 8
 MESH = pl.DeviceIdType.MESH
 
 
@@ -110,11 +110,15 @@
         single = jnp.where(me < n - 1 - me, me + far, me - far)
         return jnp.where(j <= 2 * lo, paired, single)
 
+    def step_block(j):
+        other = block_at(jnp.where(j == n, n - 1, j))
+        return jnp.where((j == 0) | (j == n - 1), me, other)
+
     def row_block(q):
         return jnp.where(q == 0, off, jnp.where(q == 1, sib, jnp.where(q == 2, cross, diag)))
 
     def obs_copy(j):
-        b = block_at(j)
+        b = step_block(j)
         cols = pl.ds(pl.multiple_of(b * rb, rb), rb)
         slot = lax.rem(j, 2)
         return (
@@ -258,63 +262,74 @@
 
     gl[...] = jnp.zeros_like(gl)
 
+    middle = has_l & has_r
+
+    def arrive_group(nxt):
+        pair = (nxt <= 2 * lo) & (lax.rem(nxt, 2) == 1)
+
+        @pl.when(pair)
+        def _():
+            near = (nxt + 1) // 2
+            arrive(me + near)
+            arrive(me - near)
+
+        @pl.when(nxt > 2 * lo)
+        def _():
+            arrive(block_at(nxt))
+
     def step(j, carry):
-        b = block_at(j)
+        b = step_block(j)
         slot = lax.rem(j, 2)
-
-        @pl.when(j < n - 1)
+        first, late, last = j == 0, j == n - 1, j == n
+
+        @pl.when(j < n)
         def _():
             for c in obs_copy(j + 1):
                 c.start()
+
+        @pl.when(j == 1)
+        def _():
+            left_copy(cross, cross, 1).wait_recv()
+            left_copy(cross, sib, 2).start()
+
+        @pl.when(jnp.logical_not(middle | first | late))
+        def _():
+            arrive(b)
 
         rbig[0:rb, :] = rcat[b]
         rbig[rb:2 * rb, 0:k] = -rcat[b, :, k:2 * k]
         rbig[rb:2 * rb, k:2 * k] = rcat[b, :, 0:k]
-        gr[b] = jnp.zeros(gr.shape[1:], jnp.float32)
+
+        @pl.when(jnp.logical_not(late))
+        def _():
+            gr[b] = jnp.zeros(gr.shape[1:], jnp.float32)
+
         for c in obs_copy(j):
             c.wait()
 
         def rows(i, carry):
             q_of = i // tiles
             t = lax.rem(i, tiles)
-            q = jnp.where(j == n - 1, 3 - q_of, q_of)
+            q = jnp.where(last, 3 - q_of, jnp.where(late, 2 + q_of, q_of))
             block = row_block(q)
 
-            @pl.when(jnp.logical_and(j == 0, t == 0))
-            def _():
-                @pl.when(q == 1)
-                def _():
-                    left_copy(sib, sib, 0).wait_recv()
-
-                @pl.when(q == 2)
-                def _():
-                    left_copy(cross, cross, 1).wait_recv()
-                    left_copy(cross, sib, 2).start()
-
-                @pl.when(q == 3)
-                def _():
-                    left_copy(diag, sib, 2).wait_recv()
-
-            @pl.when(jnp.logical_and(j < n - 1, i == 2 * tiles))
-            def _():
-                nxt = j + 1
-                pair = jnp.logical_and(nxt <= 2 * lo, lax.rem(nxt, 2) == 1)
-
-                @pl.when(pair)
-                def _():
-                    near = (nxt + 1) // 2
-                    arrive(me + near)
-                    arrive(me - near)
-
-                @pl.when(nxt > 2 * lo)
-                def _():
-                    arrive(block_at(nxt))
+            @pl.when((t == 0) & first & (q == 1))
+            def _():
+                left_copy(sib, sib, 0).wait_recv()
+
+            @pl.when((t == 0) & (j == 1) & (q == 3))
+            def _():
+                left_copy(diag, sib, 2).wait_recv()
+
+            @pl.when(middle & (j >= 1) & (j <= n - 2) & (i == 2 * tiles))
+            def _():
+                arrive_group(j + 1)
 
             at = pl.ds(pl.multiple_of(t * tr, tr), tr)
             row_at = pl.ds(pl.multiple_of(block * rb + t * tr, tr), tr)
             lrows = lfull[block, at, :]
 
-            @pl.when(j == 0)
+            @pl.when(first | ((j == 1) & (q >= 2)))
             def _():
                 turned = lrows.astype(jnp.float32).T.astype(jnp.bfloat16)
                 lt[block * tiles + t, :, 0:tr] = turned
@@ -337,7 +352,7 @@
                 lt[block * tiles + t], jnp.concatenate([miss_re, miss_im], axis=0),
                 preferred_element_type=jnp.float32)
 
-            @pl.when(jnp.logical_and(j == n - 1, t == tiles - 1))
+            @pl.when(last & (t == tiles - 1))
             def _():
                 @pl.when(q == 3)
                 def _():
@@ -348,10 +363,18 @@
                 def _():
                     asend[1], asend_s[1] = coded(gl[sib])
                     a_copy(1).start()
+                    a_copy(0).wait_recv()
+                    bsend[...], bsend_s[...] = coded(
+                        gl[cross] + arecv[0].astype(jnp.float32) * arecv_s[0])
+                    b_copy().start()
 
             return carry
 
-        lax.fori_loop(0, 4 * tiles, rows, 0)
+        lax.fori_loop(0, jnp.where(first | late, 2 * tiles, 4 * tiles), rows, 0)
+
+        @pl.when(middle & first)
+        def _():
+            arrive_group(1)
 
         @pl.when(jnp.logical_and(me == 0, b > me))
         def _():
@@ -367,11 +390,7 @@
 
         return carry
 
-    lax.fori_loop(0, n, step, 0)
-
-    a_copy(0).wait_recv()
-    bsend[...], bsend_s[...] = coded(gl[cross] + arecv[0].astype(jnp.float32) * arecv_s[0])
-    b_copy().start()
+    lax.fori_loop(0, n + 1, step, 0)
 
     def pass_on(tau, carry):
         right_t = tau - me
@@ -396,9 +415,12 @@
     lax.fori_loop(0, 2 * n, pass_on, 0)
 
     a_copy(1).wait_recv()
-    gl_out[...] = gl[off] + arecv[1].astype(jnp.float32) * arecv_s[1]
+    gl[off] += arecv[1].astype(jnp.float32) * arecv_s[1]
     b_copy().wait_recv()
-    gl_out[...] += brecv[...].astype(jnp.float32) * brecv_s[...]
+    for c in range(2):
+        part = slice(c * k, (c + 1) * k)
+        total = gl[off, :, part] + brecv[:, part].astype(jnp.float32) * brecv_s[:, part]
+        gl_out[c] = lfull[off, :, part].astype(jnp.float32) - STEP * total
 
     for p in range(PIECES):
         span = slice(p * piece, (p + 1) * piece)
@@ -413,7 +435,11 @@
             sum_arrived(n, p).wait_recv()
             gr[me, span, :] += z_received(n, p)
 
-        gr_out[:, span] = gr[me, span, :].T
+        if (p + 1) * piece % 128 == 0:
+            low = (p + 1) * piece - 128
+            c, at = low // k, slice(low % k, low % k + 128)
+            gr_out[c, :, at] = (
+                rcat[me, :, low:low + 128].astype(jnp.float32) - STEP * gr[me, low:low + 128, :].T)
 
     left_copy(off, cross, 1).wait_send()
     left_copy(off, sib, 0).wait_send()
@@ -450,17 +476,17 @@
     rb, k = left_factor.shape[1:]
     n_off = 4
     rows = rb * n_off
-    tr = min(256, rb)
+    tr = rb
     tiles = rows // tr
     dma = pltpu.SemaphoreType.DMA
     any_spec = pl.BlockSpec(memory_space=pl.ANY)
     vmem_spec = pl.BlockSpec(memory_space=pltpu.VMEM)
     bf16, f32 = jnp.bfloat16, jnp.float32
-    left_share, right_share = pl.pallas_call(
+    return pl.pallas_call(
         lambda *refs: kernel(n, rb, k, tr, *refs),
         out_shape=[
-            jax.ShapeDtypeStruct((rb, 2 * k), f32),
-            jax.ShapeDtypeStruct((rb, 2 * k), f32),
+            jax.ShapeDtypeStruct((2, rb, k), f32),
+            jax.ShapeDtypeStruct((2, rb, k), f32),
         ],
         in_specs=[any_spec] * 4,
         out_specs=[vmem_spec] * 2,
@@ -498,11 +524,6 @@
         cost_estimate=pl.CostEstimate(
             flops=24 * rows * n * rb * k, bytes_accessed=8 * rows * n * rb, transcendentals=0),
     )(observed, trace_mask, left_factor, right_factor)
-    left_share = jnp.stack([left_share[:, :k], left_share[:, k:]])
-    right_share = jnp.stack([right_share[:, :k], right_share[:, k:]])
-    left_next = left_factor.astype(f32) - STEP * left_share
-    right_next = right_factor.astype(f32) - STEP * right_share
-    return (left_next, right_next)
 
 
 def solution(mesh):

time: 94.8 us -> 83 us (0.88)
  Pallas kernels: 90.1 us -> 77.6 us
  local copies, waits for them, and re-layouts: 1.66 us -> 4.52 us
  other arithmetic: 2.23 us -> 0 us
    pallas_call x1, Pallas kernels: 90.1 us -> 77.6 us  [kernel_device(): pl.pallas_call(lambda *refs: kernel(n, rb, k, tr, *refs), out_shape=[jax....]
    unnamed x4 -> x2, local copies, waits for them, and re-layouts: 0.01 us -> 4.52 us
    sub x2 -> x0, other arithmetic: 2.23 us -> none  [the longest x1 1.12 us: kernel_device(): right_next = right_factor.astype(f32) - STEP * right_share]
    another operation x1 -> x0, local copies, waits for them, and re-layouts: 1.65 us -> none  [kernel_device(): right_share = jnp.stack([right_share[:, :k], right_share[:, k:]])]
where the time goes in v2:
time: 83 us; the launch traced here: 82.8 us
  Pallas kernels  77.6 us (93%)
  local copies, waits for them, and re-layouts  4.52 us (5%)
    pallas_call x1, Pallas kernels, kernel_device(): pl.pallas_call(lambda *refs: kernel(n, rb, k, tr, *refs), out_shape=[jax....  77.6 us
    unnamed x2, local copies, waits for them, and re-layouts  4.52 us

profile of v2, /device:TPU:0, one launch (start us, length us, event | category | flops | bytes accessed | tf_op | source)
XLA Modules:
  0.0 82.8 jit_solution(8862646249813364611)
XLA Ops:
  0.6 77.6 %shard_map.59 = (f32[2,512,256]{2,1,0:T(8,128)}, f32[2,512,256]{2,1,0:T(8,128)}) custom-call(bf16[2,2048,2048]{2,1,0:T(8,128)(2,1)} %refs_0_.1, s32[2048,2048]{1,0:T(8,128)} %refs_1_.1, bf16[2,512,256]{2,1,0:T(8,128)(2,1)} %refs_2_.1, bf16[2,512,256]{2,1,0:T(8,128)(2,1)} %refs_3_.1), custom_call_target="tpu_custom_call" | custom-call | flops 25769803776 | bytes 33554432 | tf_op jit(solution)/shard_map/pallas_call | solution.py:485
  78.2 2.3 %copy.8 = f32[2,512,256]{2,1,0:T(8,128)} copy(f32[2,512,256]{2,1,0:T(8,128)} %get-tuple-element.4) | data formatting | bytes 2097152
  80.5 2.3 %copy.9 = f32[2,512,256]{2,1,0:T(8,128)} copy(f32[2,512,256]{2,1,0:T(8,128)} %get-tuple-element.5) | data formatting | bytes 2097152

commit v3 on v2

--- a/solution.py
+++ b/solution.py
@@ -392,27 +392,29 @@
 
     lax.fori_loop(0, n + 1, step, 0)
 
-    def pass_on(tau, carry):
-        right_t = tau - me
-        left_t = 2 * (n - 1) - me - tau
-
-        @pl.when((me > 0) & (right_t > me) & (right_t < n))
-        def _():
-            for p in range(PIECES):
-                sum_arrived(right_t, p).wait_recv()
-                z_put(right_t, p, gr[right_t, p * piece:(p + 1) * piece, :] + z_received(right_t, p))
-                sum_right(right_t, p).start()
-
-        @pl.when((me < n - 1) & (left_t < me) & (left_t >= 0))
-        def _():
-            for p in range(PIECES):
-                sum_arrived(left_t, p).wait_recv()
-                z_put(left_t, p, gr[left_t, p * piece:(p + 1) * piece, :] + z_received(left_t, p))
-                sum_left(left_t, p).start()
+    def pass_on(u, carry):
+        right_v = jnp.maximum(u - me, 0)
+        left_v = jnp.maximum(u - (n - 1 - me), 0)
+        right_t, right_p = right_v // PIECES, lax.rem(right_v, PIECES)
+        left_t, left_p = n - 1 - left_v // PIECES, lax.rem(left_v, PIECES)
+
+        @pl.when((me > 0) & (u >= me) & (right_t > me) & (right_t < n))
+        def _():
+            sum_arrived(right_t, right_p).wait_recv()
+            span = pl.ds(pl.multiple_of(right_p * piece, piece), piece)
+            z_put(right_t, right_p, gr[right_t, span, :] + z_received(right_t, right_p))
+            sum_right(right_t, right_p).start()
+
+        @pl.when((me < n - 1) & (u >= n - 1 - me) & (left_t < me) & (left_t >= 0))
+        def _():
+            sum_arrived(left_t, left_p).wait_recv()
+            span = pl.ds(pl.multiple_of(left_p * piece, piece), piece)
+            z_put(left_t, left_p, gr[left_t, span, :] + z_received(left_t, left_p))
+            sum_left(left_t, left_p).start()
 
         return carry
 
-    lax.fori_loop(0, 2 * n, pass_on, 0)
+    lax.fori_loop(0, n * PIECES + n, pass_on, 0)
 
     a_copy(1).wait_recv()
     gl[off] += arecv[1].astype(jnp.float32) * arecv_s[1]

time: 83 us -> 90.8 us (1.094)
  Pallas kernels: 77.6 us -> 85.4 us
    pallas_call x1, Pallas kernels: 77.6 us -> 85.4 us  [kernel_device(): pl.pallas_call(lambda *refs: kernel(n, rb, k, tr, *refs), out_shape=[jax....]
where the time goes in v3:
time: 90.8 us; the launch traced here: 90.6 us
  Pallas kernels  85.4 us (94%)
  local copies, waits for them, and re-layouts  4.52 us (5%)
    pallas_call x1, Pallas kernels, kernel_device(): pl.pallas_call(lambda *refs: kernel(n, rb, k, tr, *refs), out_shape=[jax....  85.4 us
    unnamed x2, local copies, waits for them, and re-layouts  4.52 us

profile of v3, /device:TPU:0, one launch (start us, length us, event | category | flops | bytes accessed | tf_op | source)
XLA Modules:
  0.0 90.6 jit_solution(5567951612153352989)
XLA Ops:
  0.6 85.4 %shard_map.59 = (f32[2,512,256]{2,1,0:T(8,128)}, f32[2,512,256]{2,1,0:T(8,128)}) custom-call(bf16[2,2048,2048]{2,1,0:T(8,128)(2,1)} %refs_0_.1, s32[2048,2048]{1,0:T(8,128)} %refs_1_.1, bf16[2,512,256]{2,1,0:T(8,128)(2,1)} %refs_2_.1, bf16[2,512,256]{2,1,0:T(8,128)(2,1)} %refs_3_.1), custom_call_target="tpu_custom_call" | custom-call | flops 25769803776 | bytes 33554432 | tf_op jit(solution)/shard_map/pallas_call | solution.py:487
  86.1 2.3 %copy.8 = f32[2,512,256]{2,1,0:T(8,128)} copy(f32[2,512,256]{2,1,0:T(8,128)} %get-tuple-element.4) | data formatting | bytes 2097152
  88.3 2.3 %copy.9 = f32[2,512,256]{2,1,0:T(8,128)} copy(f32[2,512,256]{2,1,0:T(8,128)} %get-tuple-element.5) | data formatting | bytes 2097152
